TPU v7x, 256 devices: a whole 4x4x8 slice. The times are simulated.
256 devices in a mesh: row: 4 (over y), col: 64 (over z, x, core).
Axes of the slice: x: 4, y: 4, z: 8, core: 2. Of those that a mesh axis runs over, the one named last changes fastest.
Arguments:
- momentum: bfloat16 [12288, 26624], P('row', 'col'), may hold values from -120 to 120
- gradient: bfloat16 [12288, 26624], P('row', 'col'), may hold values from -120 to 120
- right_basis: float32 [26624, 512], P('col'), may hold values from -0.0390625 to 0.0390625
Outputs:
- new_momentum: bfloat16 [12288, 26624], P('row', 'col')
- new_basis: float32 [26624, 512], P('col')
- direction: bfloat16 [12288, 26624], P('row', 'col')
All inputs are finite; a program needn't handle non-finite values.
Results may differ from a plain program's by a relative error of at most 0.024.
Values may be sent and summed in bfloat16 or wider, within the bound.
No kernel may reach another device: no remote copies, remote signals or barrier semaphores. Data moves between devices by JAX's collectives and lax.ppermute only.
A program may use at most 128 MiB of HBM per device.

v0:
```python
import math

import jax
import jax.numpy as jnp
from jax import lax
from jax.sharding import PartitionSpec as P

D = 12288
FF = 26624
RANK = 512


error_share = 0.05
epsilon = 1e-06


def gram_of(block):
    return jnp.einsum(
        "dr,ds->rs",
        block,
        block,
        precision=lax.Precision.HIGHEST,
        preferred_element_type=jnp.float32,
    )


def orthonormalize(block, gram_matrix):
    chol_factor = jnp.linalg.cholesky(gram_matrix)
    solved = lax.linalg.triangular_solve(
        chol_factor, block, left_side=False, lower=True, transpose_a=True
    )
    return solved.astype(jnp.bfloat16)


def shards(momentum, gradient, right_basis):
    blended = (momentum.astype(jnp.float32) + gradient.astype(jnp.float32)).astype(jnp.bfloat16)
    basis_half = right_basis.astype(jnp.bfloat16)
    partial_proj = jnp.dot(blended, basis_half, preferred_element_type=jnp.float32)
    projected = lax.psum(partial_proj, "col")
    gram_matrix = lax.psum(gram_of(projected).astype(jnp.bfloat16), "row").astype(jnp.float32)
    ortho_half = orthonormalize(projected, gram_matrix)
    partial_back = jnp.einsum("dk,dr->kr", blended, ortho_half, preferred_element_type=jnp.float32)
    back_proj = lax.psum(partial_back.astype(jnp.bfloat16), "row").astype(jnp.float32)
    back_half = back_proj.astype(jnp.bfloat16)
    low_rank = jnp.einsum("dr,kr->dk", ortho_half, back_half, preferred_element_type=jnp.float32)
    new_momentum = (blended.astype(jnp.float32) - error_share * low_rank).astype(jnp.bfloat16)
    col_sq = lax.psum(jnp.sum(back_proj * back_proj, axis=0), "col")
    new_basis = back_proj / (jnp.sqrt(col_sq) + epsilon)
    scale_factor = math.sqrt(D * FF / RANK)
    product = jnp.einsum(
        "dr,kr->dk", ortho_half, new_basis.astype(jnp.bfloat16), preferred_element_type=jnp.float32
    )
    direction = (product * scale_factor).astype(jnp.bfloat16)
    return (new_momentum, new_basis, direction)


def solution(mesh):
    in_specs = (P("row", "col"), P("row", "col"), P("col", None))
    out_specs = (P("row", "col"), P("col", None), P("row", "col"))
    return jax.shard_map(shards, mesh=mesh, in_specs=in_specs, out_specs=out_specs, check_vma=False)
```

profile of v0, /device:TPU:8, one launch (start us, length us, event | category | flops | bytes accessed | tf_op | source)
XLA Modules:
  0.0 634.8 jit_solution(3446376350069480338)
XLA Ops:
  7.2 7.2 %fusion.17 = f32[3072,512]{1,0:T(8,128)} fusion(f32[416,512]{1,0:T(8,128)} %param.5, bf16[3072,416]{0,1:T(8,128)(2,1)} %param.4, bf16[3072,416]{0,1:T(8,128)(2,1)} %param.3), kind=kOutput, calls=%fused_computation.36 | convolution fusion | flops 1313947648 | bytes 12255232 | tf_op jit(solution)/shard_map/dot_general | solution.py:38
  14.5 203.4 %all-reduce.5.cloned.1.call-done = f32[3072,512]{1,0:T(8,128)} async-done(((f32[3072,512]{1,0:T(8,128)}), f32[3072,512]{1,0:T(8,128)}) %all-reduce.5.cloned.1.call-update) | async-done | bytes 6291472 | tf_op jit(solution)/shard_map/psum | solution.py:39
  217.9 14.8 %convolution_convert_fusion.1 = bf16[512,512]{0,1:T(8,128)(2,1)} fusion(f32[3072,512]{1,0:T(8,128)} %all-reduce.5.cloned.1.call-done), kind=kOutput, calls=%fused_computation.21 | convolution fusion | flops 9663938560 | bytes 6815744 | tf_op jit(solution)/shard_map/dr,ds->rs/dot_general | solution.py:18
  233.0 45.8 %all-reduce.7.cloned.1.call-done = bf16[512,512]{0,1:T(8,128)(2,1)} async-done(((bf16[512,512]{0,1:T(8,128)(2,1)}), bf16[512,512]{0,1:T(8,128)(2,1)}) %all-reduce.7.cloned.1.call-update) | async-done | bytes 524304 | tf_op jit(solution)/shard_map/psum | solution.py:40
  281.3 11.7 %cholesky.104 = f32[128,128]{1,0:T(8,128)S(1)} custom-call(f32[128,128]{1,0:T(8,128)S(1)} %cholesky.266), custom_call_target="Cholesky" | custom-call | tf_op jit(solution)/shard_map/jit(cholesky)/cholesky | solution.py:28
  293.0 9.8 %custom-call.30 = f32[1,128,128]{1,2,0:T(8,128)S(1)} custom-call(f32[1,128,128]{2,1,0:T(8,128)S(1)} %get-tuple-element.30), custom_call_target="InvertDiagBlocksLowerTriangular" | custom-call | tf_op jit(solution)/shard_map/jit(cholesky)/cholesky | solution.py:28
  303.6 11.7 %cholesky.217 = f32[128,128]{1,0:T(8,128)S(1)} custom-call(f32[128,128]{1,0:T(8,128)S(1)} %cholesky.270), custom_call_target="Cholesky" | custom-call | tf_op jit(solution)/shard_map/jit(cholesky)/cholesky | solution.py:28
  315.4 10.2 %custom-call.31 = f32[1,128,128]{1,2,0:T(8,128)S(1)} custom-call(f32[1,128,128]{2,1,0:T(8,128)S(1)} %get-tuple-element.27), custom_call_target="InvertDiagBlocksLowerTriangular" | custom-call | tf_op jit(solution)/shard_map/jit(cholesky)/cholesky | solution.py:28
  326.2 11.7 %cholesky.238 = f32[128,128]{1,0:T(8,128)S(1)} custom-call(f32[128,128]{1,0:T(8,128)S(1)} %cholesky.275), custom_call_target="Cholesky" | custom-call | tf_op jit(solution)/shard_map/jit(cholesky)/cholesky | solution.py:28
  338.6 9.8 %custom-call.32 = f32[1,128,128]{1,2,0:T(8,128)S(1)} custom-call(f32[1,128,128]{2,1,0:T(8,128)S(1)} %get-tuple-element.24), custom_call_target="InvertDiagBlocksLowerTriangular" | custom-call | tf_op jit(solution)/shard_map/jit(cholesky)/cholesky | solution.py:28
  349.0 11.7 %cholesky.255 = f32[128,128]{1,0:T(8,128)S(1)} custom-call(f32[128,128]{1,0:T(8,128)S(1)} %convolution_subtract_fusion.4), custom_call_target="Cholesky" | custom-call | tf_op jit(solution)/shard_map/jit(cholesky)/cholesky | solution.py:28
  364.8 8.0 %while.1 = (s32[]{:T(128)}, f32[512,512]{1,0:T(8,128)S(1)}, s32[4,2]{0,1:T(2,128)S(1)}, f32[4,128,128]{2,1,0:T(8,128)S(1)}, s32[]{:T(128)}) while((s32[]{:T(128)}, f32[512,512]{1,0:T(8,128)S(1)}, s32[4,2]{0,1:T(2,128)S(1)}, f32[4,128,128]{2,1,0:T(8,128)S(1)}, s32[]{:T(128)}) %tuple.34), condition=%wide.while_cond, body=%wide.while_body.sunk | while | flops 2 | bytes 131189 | solution.py:29
  372.8 39.5 %custom-call.33 = f32[4,128,128]{1,2,0:T(8,128)S(1)} custom-call(f32[4,128,128]{2,1,0:T(8,128)S(1)} %get-tuple-element.10), custom_call_target="InvertDiagBlocksLowerTriangular" | custom-call | tf_op jit(solution)/shard_map/triangular_solve | solution.py:29
  412.3 3.1 fusion.40
  415.4 4.4 convolution_subtract_fusion
  421.4 5.4 convolution_subtract_fusion.1
  426.8 1.8 fusion.38
  428.6 9.3 %fusion.6 = f32[3072,128]{1,0:T(8,128)S(1)} fusion(f32[3072,128]{0,1:T(8,128)S(1)} %get-tuple-element.34, f32[3072,128]{0,1:T(8,128)S(1)} %get-tuple-element.36, f32[3072,128]{0,1:T(8,128)S(1)} %get-tuple-element.38, f32[3072,512]{1,0:T(8,128)S(1)} %bitcast.58, f32[512,512]{1,0:T(8,128)} %copy-done.3), kind=kOutput, calls=%fused_computation.13 | convolution fusion | flops 1814691840 | bytes 8060928 | tf_op jit(solution)/shard_map/triangular_solve | solution.py:29
  437.9 2.4 convolution_convert_fusion
  440.4 2.3 convolution_convert_fusion.2
  442.7 48.2 %all-reduce.9.cloned.1.call-done = bf16[416,512]{1,0:T(8,128)(2,1)} async-done(((bf16[416,512]{1,0:T(8,128)(2,1)}), bf16[416,512]{1,0:T(8,128)(2,1)}) %all-reduce.9.cloned.1.call-update) | async-done | bytes 426000 | tf_op jit(solution)/shard_map/psum | solution.py:43
  492.1 127.0 %psum.31 = f32[512]{0:T(512)S(1)} all-reduce(f32[512]{0:T(512)S(1)} %fusion.15), channel_id=1, replica_groups=mesh['row'=4,'col'=64] {'col'}, use_global_device_ids=true, to_apply=%region_12.13 | all-reduce | flops 512 | bytes 4096 | tf_op jit(solution)/shard_map/psum | solution.py:47
  620.2 4.9 multiply_convert_fusion
  625.2 2.9 subtract_convert_fusion
  (76 shorter events, 18.9 us)
Async XLA Ops:
  7.2 210.7 %all-reduce.5.cloned.1.call-start = ((), (), s32[]{:S(2)}) async-start(), calls=%async_computation | async-start | bytes 12582912 | tf_op jit(solution)/shard_map/psum | solution.py:39
  14.5 264.3 %all-reduce.7.cloned.1.call-start = ((), (), s32[]{:S(2)}) async-start(), calls=%async_computation.1 | async-start | bytes 1048576 | tf_op jit(solution)/shard_map/psum | solution.py:40
  232.7 258.2 %all-reduce.9.cloned.1.call-start = ((), (), s32[]{:S(2)}) async-start(), calls=%async_computation.2 | async-start | bytes 851968 | tf_op jit(solution)/shard_map/psum | solution.py:43
  372.8 48.6 %copy-start.3 = (f32[512,512]{1,0:T(8,128)}, f32[512,512]{1,0:T(8,128)S(1)}, u32[]{:S(2)}) copy-start(f32[512,512]{1,0:T(8,128)S(1)} %get-tuple-element.91) | copy-start | bytes 3145732
  412.3 14.5 %copy-start.12 = (f32[4,128,128]{1,2,0:T(8,128)}, f32[4,128,128]{1,2,0:T(8,128)S(1)}, u32[]{:S(2)}) copy-start(f32[4,128,128]{1,2,0:T(8,128)S(1)} %custom-call.33) | copy-start | bytes 786436
  412.3 9.1 %slice-start = ((s8[6291456]{0:T(1024)(128)(4,1)}), s8[4194304]{0:T(1024)(128)(4,1)S(1)}, s32[]{:S(2)}) async-start(s8[6291456]{0:T(1024)(128)(4,1)} %bitcast.57), calls=%async_computation.3 | async-start | bytes 8388608
  415.4 24.9 %copy-start.6 = (bf16[3072,128]{0,1:T(8,128)(2,1)}, bf16[3072,128]{0,1:T(8,128)(2,1)S(1)}, u32[]{:S(2)}) copy-start(bf16[3072,128]{0,1:T(8,128)(2,1)S(1)} %get-tuple-element.37) | copy-start | bytes 2359300
  415.4 6.0 slice-start.1
  421.4 19.0 %copy-start.8 = (bf16[3072,128]{0,1:T(8,128)(2,1)}, bf16[3072,128]{0,1:T(8,128)(2,1)S(1)}, u32[]{:S(2)}) copy-start(bf16[3072,128]{0,1:T(8,128)(2,1)S(1)} %get-tuple-element.35) | copy-start | bytes 2359300
  428.6 11.8 %copy-start.10 = (bf16[3072,128]{0,1:T(8,128)(2,1)}, bf16[3072,128]{0,1:T(8,128)(2,1)S(1)}, u32[]{:S(2)}) copy-start(bf16[3072,128]{0,1:T(8,128)(2,1)S(1)} %get-tuple-element.33) | copy-start | bytes 2359300
  428.6 11.8 %copy-start = (bf16[3072,416]{0,1:T(8,128)(2,1)S(1)}, bf16[3072,416]{0,1:T(8,128)(2,1)}, u32[]{:S(2)}) copy-start(bf16[3072,416]{0,1:T(8,128)(2,1)} %param.4) | copy-start | bytes 7667716
  428.6 11.8 %copy-start.1 = (bf16[3072,416]{0,1:T(8,128)(2,1)S(1)}, bf16[3072,416]{0,1:T(8,128)(2,1)}, u32[]{:S(2)}) copy-start(bf16[3072,416]{0,1:T(8,128)(2,1)} %param.3) | copy-start | bytes 7667716
  620.2 5.0 copy-start.5
  620.2 5.0 copy-start.2
  620.2 5.0 copy-start.4
  620.2 5.0 copy-start.7
  620.2 5.0 copy-start.9
  620.2 5.0 copy-start.11
Sparse Core Ops, SparseCore 0:
  14.6 203.2 all-reduce.4
  232.9 45.8 all-reduce.6
  442.8 48.0 all-reduce.8
where the time goes:
time: 640 us; the launch traced here: 635 us
  waiting for transfers between devices  297 us (46%)
  blocking collectives  127 us (20%)
  other arithmetic  122 us (19%)
  matrix products  61.9 us (10%)
  between operations  16.9 us (3%)
  local copies, waits for them, and re-layouts  9.39 us (1%)
    psum x1, waiting for transfers between devices, shards(): projected = lax.psum(partial_proj, 'col')  203 us
    psum x1, blocking collectives, shards(): col_sq = lax.psum(jnp.sum(back_proj * back_proj, axis=0), 'col')  127 us
    another operation x14, other arithmetic, orthonormalize(): chol_factor = jnp.linalg.cholesky(gram_matrix)  78.7 us
    psum x1, waiting for transfers between devices, shards(): lax.psum(partial_back.astype(jnp.bfloat16), 'row').astype(jnp.float32)  48.2 us
    psum x1, waiting for transfers between devices, shards(): lax.psum(gram_of(projected).astype(jnp.bfloat16), 'row').astype(jnp.float32)  45.8 us
    another operation x3, other arithmetic, orthonormalize(): lax.linalg.triangular_solve(chol_factor, block, left_side=False, lower=Tr...  39.6 us
    another operation x7, matrix products, orthonormalize(): lax.linalg.triangular_solve(chol_factor, block, left_side=False, lower=Tr...  27.9 us
    dot_general x1, matrix products, gram_of(): jnp.einsum('dr,ds->rs', block, block, precision=lax.Precision.HIGHEST, pr...  14.8 us
  transfers between devices with their start and end apart: 3, of which 3 were waited for; matrix products, arithmetic and copies ran while one was open for 0% of the time, Pallas kernels for 0%

commit v1 on v0

v1 whole, which is shorter than its diff:
```python
import math

import jax
import jax.numpy as jnp
from jax import lax
from jax.experimental import pallas as pl
from jax.experimental.pallas import tpu as pltpu
from jax.sharding import Mesh
from jax.sharding import PartitionSpec as P

RANK = 512
NB = 128
HI = lax.Precision.HIGHEST
F32 = jnp.float32
BF16 = jnp.bfloat16
error_share = 0.05
epsilon = 1e-06


def factor_block(d_ref, x_ref, sub):
    groups = NB // 8
    wide = (8, NB)
    for b in range(groups):
        r0 = 8 * b
        rows_d = d_ref[r0 : r0 + 8, :]
        rows_x = x_ref[r0 : r0 + 8, :]
        cols = [jnp.broadcast_to(rows_d[:, r0 + j : r0 + j + 1], wide) for j in range(8)]
        pivots = jnp.ones(wide, F32)
        row_d, row_x, inverse, coef = [], [], [], {}
        for k in range(8):
            pivot = jnp.broadcast_to(cols[k][k : k + 1, :], wide)
            recip = 1.0 / pivot
            pivots = jnp.where(sub == k, pivot, pivots)
            dk = jnp.broadcast_to(rows_d[k : k + 1, :], wide)
            xk = jnp.broadcast_to(rows_x[k : k + 1, :], wide)
            factor = jnp.where(sub > k, cols[k] * recip, 0.0)
            for j in range(k + 1, 8):
                coef[k, j] = jnp.broadcast_to(cols[j][k : k + 1, :], wide)
                cols[j] = cols[j] - factor * coef[k, j]
            rows_d = rows_d - factor * dk
            rows_x = rows_x - factor * xk
            row_d.append(dk)
            row_x.append(xk)
            inverse.append(recip)
        x_ref[r0 : r0 + 8, :] = rows_x * lax.rsqrt(pivots)
        for v in range(b + 1, groups):
            q = 8 * v
            low_d = d_ref[q : q + 8, :]
            low_x = x_ref[q : q + 8, :]
            lead = [jnp.broadcast_to(low_d[:, r0 + j : r0 + j + 1], wide) for j in range(8)]
            for k in range(8):
                factor = lead[k] * inverse[k]
                for j in range(k + 1, 8):
                    lead[j] = lead[j] - factor * coef[k, j]
                low_d = low_d - factor * row_d[k]
                low_x = low_x - factor * row_x[k]
            d_ref[q : q + 8, :] = low_d
            x_ref[q : q + 8, :] = low_x


def eye(size):
    row = lax.broadcasted_iota(jnp.int32, (size, size), 0)
    col = lax.broadcasted_iota(jnp.int32, (size, size), 1)
    return jnp.where(row == col, 1.0, 0.0).astype(F32)


def chol_kernel(g_ref, o_ref, a_ref, d_ref, x_ref):
    sub = lax.broadcasted_iota(jnp.int32, (8, NB), 0)
    a_ref[...] = g_ref[...]
    o_ref[...] = eye(RANK)
    lane = lax.broadcasted_iota(jnp.int32, (NB, RANK), 1)

    def step(p, carry):
        at = pl.multiple_of(p * NB, NB)
        rows = pl.ds(at, NB)
        d_ref[...] = a_ref[rows, rows]
        x_ref[...] = eye(NB)
        factor_block(d_ref, x_ref, sub)
        block = x_ref[...]
        upper = jnp.dot(block, a_ref[rows, :], precision=HI, preferred_element_type=F32)
        done = jnp.dot(block, o_ref[rows, :], precision=HI, preferred_element_type=F32)
        o_ref[rows, :] = done
        below = jnp.where(lane >= at + NB, upper, 0.0)
        dims = (((0,), (0,)), ((), ()))
        a_ref[...] -= lax.dot_general(below, upper, dims, precision=HI, preferred_element_type=F32)
        o_ref[...] -= lax.dot_general(below, done, dims, precision=HI, preferred_element_type=F32)
        return carry

    lax.fori_loop(0, RANK // NB, step, 0)


def inverse_factor(gram):
    return pl.pallas_call(
        chol_kernel,
        out_shape=jax.ShapeDtypeStruct((RANK, RANK), F32),
        scratch_shapes=[
            pltpu.VMEM((RANK, RANK), F32),
            pltpu.VMEM((NB, NB), F32),
            pltpu.VMEM((NB, NB), F32),
        ],
        compiler_params=pltpu.CompilerParams(vmem_limit_bytes=24 * 1024 * 1024),
        cost_estimate=pl.CostEstimate(flops=20_000_000_000, bytes_accessed=2 * RANK * RANK * 4, transcendentals=0),
        name="inverse_factor",
    )(gram)


def swap(block, axis):
    return lax.all_to_all(block, axis, 0, 0, tiled=True)


def scatter_sum(block, axis, n):
    rows = block.shape[0] // n
    got = swap(block.reshape(n, rows, RANK), axis)
    return jnp.sum(got.astype(F32), axis=0).astype(BF16)


def gather(block, axis, n):
    got = swap(jnp.broadcast_to(block[None], (n, *block.shape)), axis)
    return got.reshape(n * block.shape[0], RANK)


def shift(value, axis, n, by):
    return lax.ppermute(value, axis, [(i, (i + by) % n) for i in range(n)])


def row_sum(block, n):
    me = lax.axis_index("row")
    rows = block.shape[0] // n
    pieces = block.reshape(n, rows, RANK)
    piece = lambda i: lax.dynamic_index_in_dim(pieces, lax.rem(i, n), 0, keepdims=False)
    total = piece(me).astype(F32)
    for by in range(1, n):
        total = total + shift(piece(me + by), "row", n, by).astype(F32)
    mine = total.astype(BF16)
    held = jnp.stack([mine] + [shift(mine, "row", n, by) for by in range(1, n)])
    return jnp.concatenate(
        [lax.dynamic_index_in_dim(held, lax.rem(me - i + n, n), 0, keepdims=False) for i in range(n)]
    )


def butterfly(value, sizes):
    for axis, n in sizes:
        step = 1
        while step < n:
            value = value + lax.ppermute(value, axis, [(i, i ^ step) for i in range(n)])
            step *= 2
    return value


def shards(sizes, whole, momentum, gradient, right_basis):
    core = lax.axis_index("core")
    blended = (momentum.astype(F32) + gradient.astype(F32)).astype(BF16)
    basis_half = right_basis.astype(BF16)
    part = jnp.dot(blended, basis_half, preferred_element_type=F32).astype(BF16)
    for axis in ("core", "x", "z"):
        part = scatter_sum(part, axis, sizes[axis])
    for axis in ("z", "x"):
        part = gather(part, axis, sizes[axis])
    other = shift(part, "core", 2, 1)
    gram_part = lax.dot_general(part, part, (((0,), (0,)), ((), ())), preferred_element_type=F32).astype(BF16)
    both = ("row", "core")
    gram = gather(scatter_sum(gram_part, both, sizes["row"] * 2), both, sizes["row"] * 2).astype(F32)
    first = core == 0
    projected = jnp.concatenate([jnp.where(first, part, other), jnp.where(first, other, part)])
    cross = lax.dot_general(blended, projected, (((0,), (0,)), ((), ())), preferred_element_type=F32)
    cross = row_sum(cross.astype(BF16), sizes["row"])
    inverse = inverse_factor(gram).astype(BF16)
    times = (((1,), (1,)), ((), ()))
    back_proj = lax.dot_general(cross, inverse, times, preferred_element_type=F32)
    col_sq = jnp.sum(back_proj * back_proj, axis=0, keepdims=True)
    col_sq = butterfly(col_sq, [(axis, sizes[axis]) for axis in ("core", "x", "z")])
    ortho_half = lax.dot_general(projected, inverse, times, preferred_element_type=F32).astype(BF16)
    back_half = back_proj.astype(BF16)
    low_rank = lax.dot_general(ortho_half, back_half, times, preferred_element_type=F32)
    new_momentum = (blended.astype(F32) - error_share * low_rank).astype(BF16)
    new_basis = back_proj / (jnp.sqrt(col_sq) + epsilon)
    product = lax.dot_general(ortho_half, new_basis.astype(BF16), times, preferred_element_type=F32)
    direction = (product * math.sqrt(whole / RANK)).astype(BF16)
    return (new_momentum, new_basis, direction)


def solution(mesh):
    sizes = {"row": 4, "z": 8, "x": 4, "core": 2}
    inner = Mesh(mesh.devices.reshape(tuple(sizes.values())), tuple(sizes))
    col = ("z", "x", "core")

    def step(momentum, gradient, right_basis):
        whole = momentum.shape[0] * momentum.shape[1]
        body = lambda *args: shards(sizes, whole, *args)
        return jax.shard_map(
            body,
            mesh=inner,
            in_specs=(P("row", col), P("row", col), P(col, None)),
            out_specs=(P("row", col), P(col, None), P("row", col)),
            check_vma=False,
        )(momentum, gradient, right_basis)

    return step
```

time: 640 us -> 192 us (0.30)
  waiting for transfers between devices: 297 us -> 30.4 us
  other arithmetic: 122 us -> 4.92 us
  matrix products: 61.9 us -> 16.4 us
  blocking collectives: 127 us -> 88.8 us
  Pallas kernels: 0 us -> 25.5 us
  starting transfers between devices: 0.3 us -> 22.2 us
  between operations: 16.9 us -> 0.85 us
  local copies, waits for them, and re-layouts: 9.39 us -> 2.77 us
    psum x3 -> x0, waiting for transfers between devices: 297 us -> none  [the longest x1 203 us: shards(): projected = lax.psum(partial_proj, 'col')]
    psum x1 -> x0, blocking collectives: 127 us -> none  [shards(): col_sq = lax.psum(jnp.sum(back_proj * back_proj, axis=0), 'col')]
    another operation x17 -> x1, other arithmetic: 118 us -> 0.06 us  [row_sum(): held = jnp.stack([mine] + [shift(mine, 'row', n, by) for by in range(1, n)])]
    all_to_all x0 -> x5, blocking collectives: none -> 88.8 us  [swap(): return lax.all_to_all(block, axis, 0, 0, tiled=True)]
    another operation x13 -> x0, matrix products: 29.8 us -> none  [the longest x7 27.9 us: orthonormalize(): lax.linalg.triangular_solve(chol_factor, block, left_side=False, lower=Tr...]
    pallas_call x0 -> x1, Pallas kernels: none -> 25.5 us  [inverse_factor(): pl.pallas_call(chol_kernel, out_shape=jax.ShapeDtypeStruct((RANK, RANK),...]
    ppermute x0 -> x13, waiting for transfers between devices: none -> 21.5 us  [the longest x6 16.6 us: butterfly(): value = value + lax.ppermute(value, axis, [(i, i ^ step) for i in range(n)])]
    dot_general x5 -> x7, matrix products: 32.2 us -> 16.4 us  [the longest x1 4.59 us: shards(): part = jnp.dot(blended, basis_half, preferred_element_type=F32).astype(BF16)]
  transfers between devices with their start and end apart: 3 -> 15, of which waited for: 3 -> 10; matrix products, arithmetic and copies ran while one was open for 0% -> 6% of each run, Pallas kernels for 0% -> 13%
where the time goes in v1:
time: 192 us
  blocking collectives  88.8 us (46%)
  waiting for transfers between devices  30.4 us (16%)
  Pallas kernels  25.5 us (13%)
  starting transfers between devices  22.2 us (12%)
  matrix products  16.4 us (9%)
  other arithmetic  4.92 us (3%)
  local copies, waits for them, and re-layouts  2.77 us (1%)
    all_to_all x5, blocking collectives, swap(): return lax.all_to_all(block, axis, 0, 0, tiled=True)  88.8 us
    pallas_call x1, Pallas kernels, inverse_factor(): pl.pallas_call(chol_kernel, out_shape=jax.ShapeDtypeStruct((RANK, RANK),...  25.5 us
    ppermute x6, waiting for transfers between devices, butterfly(): value = value + lax.ppermute(value, axis, [(i, i ^ step) for i in range(n)])  16.6 us
    all_to_all x2, starting transfers between devices, swap(): return lax.all_to_all(block, axis, 0, 0, tiled=True)  9.89 us
    all_to_all x2, waiting for transfers between devices, swap(): return lax.all_to_all(block, axis, 0, 0, tiled=True)  8.89 us
    ppermute x7, starting transfers between devices, shift(): return lax.ppermute(value, axis, [(i, (i + by) % n) for i in range(n)])  8.5 us
    ppermute x7, waiting for transfers between devices, shift(): return lax.ppermute(value, axis, [(i, (i + by) % n) for i in range(n)])  4.84 us
    dot_general x1, matrix products, shards(): part = jnp.dot(blended, basis_half, preferred_element_type=F32).astype(BF16)  4.59 us
  transfers between devices with their start and end apart: 15, of which 10 were waited for; matrix products, arithmetic and copies ran while one was open for 6% of the time, Pallas kernels for 13%

profile of v1, /device:TPU:8, one launch (start us, length us, event | category | flops | bytes accessed | tf_op | source)
XLA Modules:
  0.0 191.8 jit_solution(12335097828250101537)
XLA Ops:
  0.6 4.6 %convolution_convert_fusion.1 = bf16[3072,512]{1,0:T(8,128)(2,1)S(1)} fusion(f32[416,512]{1,0:T(8,128)} %param.5, bf16[3072,416]{0,1:T(8,128)(2,1)} %param.4, bf16[3072,416]{0,1:T(8,128)(2,1)} %param.3), kind=kOutput, calls=%fused_computation.4 | convolution fusion | flops 1315520512 | bytes 9109504 | tf_op jit(solution)/shard_map/dot_general | solution.py:154
  5.2 6.3 %all_to_all.35 = bf16[2,1536,512]{2,1,0:T(8,128)(2,1)S(1)} all-to-all(bf16[2,1536,512]{2,1,0:T(8,128)(2,1)S(1)} %bitcast.45), channel_id=1, replica_groups=mesh['row'=4,'z'=8,'x'=4,'core'=2] {'core'}, dimensions={0} | all-to-all | bytes 6291456 | tf_op jit(solution)/shard_map/all_to_all | solution.py:108
  11.5 2.2 %reduce_sum.57 = bf16[1536,512]{1,0:T(8,128)(2,1)} reduce(bf16[2,1536,512]{2,1,0:T(8,128)(2,1)S(1)} %all_to_all.35, bf16[]{:T(256)} %constant.62.clone.1), dimensions={0}, to_apply=%region_0.0 | reduce | flops 786432 | bytes 4718594 | tf_op jit(solution)/shard_map/reduce_sum | solution.py:114
  13.7 25.3 %all_to_all.36 = bf16[4,384,512]{2,1,0:T(8,128)(2,1)S(1)} all-to-all(bf16[4,384,512]{2,1,0:T(8,128)(2,1)} %bitcast.44), channel_id=1, replica_groups=mesh['row'=4,'z'=8,'x'=4,'core'=2] {'x'}, dimensions={0} | all-to-all | bytes 3145728 | tf_op jit(solution)/shard_map/all_to_all | solution.py:108
  39.4 21.8 %all_to_all.37 = bf16[8,48,512]{2,1,0:T(8,128)(2,1)S(1)} all-to-all(bf16[8,48,512]{2,1,0:T(8,128)(2,1)S(1)} %bitcast.46), channel_id=1, replica_groups=mesh['row'=4,'z'=8,'x'=4,'core'=2] {'z'}, dimensions={0} | all-to-all | bytes 786432 | tf_op jit(solution)/shard_map/all_to_all | solution.py:108
  61.3 15.4 %all_to_all.38 = bf16[8,48,512]{2,1,0:T(8,128)(2,1)S(1)} all-to-all(bf16[8,48,512]{2,1,0:T(8,128)(2,1)S(1)} %broadcast_in_dim.10), channel_id=1, replica_groups=mesh['row'=4,'z'=8,'x'=4,'core'=2] {'z'}, dimensions={0} | all-to-all | bytes 786432 | tf_op jit(solution)/shard_map/all_to_all | solution.py:108
  76.9 20.0 %all_to_all.39 = bf16[4,384,512]{2,1,0:T(8,128)(2,1)S(1)} all-to-all(bf16[4,384,512]{2,1,0:T(8,128)(2,1)S(1)} %broadcast_in_dim.24), channel_id=1, replica_groups=mesh['row'=4,'z'=8,'x'=4,'core'=2] {'x'}, dimensions={0} | all-to-all | bytes 3145728 | tf_op jit(solution)/shard_map/all_to_all | solution.py:108
  96.8 1.8 fusion.1
  98.6 5.0 %all-to-all-start.5 = ((bf16[8,64,512]{2,1,0:T(8,128)(2,1)}), bf16[8,64,512]{2,1,0:T(8,128)(2,1)S(1)}, u32[]{:S(2)}, u32[]{:S(2)}) async-start(bf16[8,64,512]{2,1,0:T(8,128)(2,1)} %bitcast.6), calls=%async_computation.5 | async-start | bytes 1048576 | tf_op jit(solution)/shard_map/all_to_all | solution.py:108
  103.7 8.9 %all-to-all-done.5 = bf16[8,64,512]{2,1,0:T(8,128)(2,1)S(1)} async-done(((bf16[8,64,512]{2,1,0:T(8,128)(2,1)}), bf16[8,64,512]{2,1,0:T(8,128)(2,1)S(1)}, u32[]{:S(2)}, u32[]{:S(2)}) %all-to-all-start.5) | async-done | bytes 524320 | tf_op jit(solution)/shard_map/all_to_all | solution.py:108
  113.5 4.9 %all-to-all-start.6 = ((bf16[8,64,512]{2,1,0:T(8,128)(2,1)}), bf16[8,64,512]{2,1,0:T(8,128)(2,1)S(1)}, u32[]{:S(2)}, u32[]{:S(2)}) async-start(bf16[8,64,512]{2,1,0:T(8,128)(2,1)} %broadcast_in_dim.25), calls=%async_computation.6 | async-start | bytes 1048576 | tf_op jit(solution)/shard_map/all_to_all | solution.py:108
  125.5 2.1 %collective-permute-start.2 = (bf16[104,512]{1,0:T(8,128)(2,1)S(1)}, bf16[104,512]{1,0:T(8,128)(2,1)S(1)}, u32[]{:S(2)}, u32[]{:S(2)}) collective-permute-start(bf16[104,512]{1,0:T(8,128)(2,1)S(1)} %get-tuple-element.11), channel_id=1, source_target_pairs={{0,128},{64,192},{128,0},{192,64},{1,129},{65,193},{129,1},{193,65... | collective-permute-start | bytes 319496 | tf_op jit(solution)/shard_map/ppermute | solution.py:123
  130.1 2.4 %collective-permute-done.2 = bf16[104,512]{1,0:T(8,128)(2,1)S(1)} collective-permute-done((bf16[104,512]{1,0:T(8,128)(2,1)S(1)}, bf16[104,512]{1,0:T(8,128)(2,1)S(1)}, u32[]{:S(2)}, u32[]{:S(2)}) %collective-permute-start.2) | collective-permute-done | bytes 106528 | tf_op jit(solution)/shard_map/ppermute | solution.py:123
  134.8 2.2 %collective-permute-start.4 = (bf16[104,512]{1,0:T(8,128)(2,1)S(1)}, bf16[104,512]{1,0:T(8,128)(2,1)S(1)}, u32[]{:S(2)}, u32[]{:S(2)}) collective-permute-start(bf16[104,512]{1,0:T(8,128)(2,1)S(1)} %fusion.18), channel_id=1, source_target_pairs={{0,64},{64,128},{128,192},{192,0},{1,65},{65,129},{129,193},{193,1... | collective-permute-start | bytes 319496 | tf_op jit(solution)/shard_map/ppermute | solution.py:123
  136.9 25.5 %inverse_factor.1 = f32[512,512]{1,0:T(8,128)S(1)} custom-call(f32[512,512]{1,0:T(8,128)S(1)} %bitcast_convert_fusion.g_ref), custom_call_target="tpu_custom_call" | custom-call | flops 20000000000 | bytes 2097152 | tf_op jit(solution)/shard_map/inverse_factor/pallas_call | solution.py:93
  164.9 3.0 %collective-permute-done.8 = f32[1,512]{1,0:T(1,128)S(1)} collective-permute-done((f32[1,512]{1,0:T(1,128)S(1)}, f32[1,512]{1,0:T(1,128)S(1)}, u32[]{:S(2)}, u32[]{:S(2)}) %collective-permute-start.8) | collective-permute-done | bytes 2080 | tf_op jit(solution)/shard_map/ppermute | solution.py:145
  168.7 4.2 %collective-permute-done.9 = f32[1,512]{1,0:T(1,128)S(1)} collective-permute-done((f32[1,512]{1,0:T(1,128)S(1)}, f32[1,512]{1,0:T(1,128)S(1)}, u32[]{:S(2)}, u32[]{:S(2)}) %collective-permute-start.9) | collective-permute-done | bytes 2080 | tf_op jit(solution)/shard_map/ppermute | solution.py:145
  173.1 3.5 %collective-permute-done.10 = f32[1,512]{1,0:T(1,128)S(1)} collective-permute-done((f32[1,512]{1,0:T(1,128)S(1)}, f32[1,512]{1,0:T(1,128)S(1)}, u32[]{:S(2)}, u32[]{:S(2)}) %collective-permute-start.10) | collective-permute-done | bytes 2080 | tf_op jit(solution)/shard_map/ppermute | solution.py:145
  176.8 1.9 %convolution_convert_fusion = bf16[3072,512]{1,0:T(8,128)(2,1)S(1)} fusion(bf16[1536,512]{1,0:T(8,128)(2,1)S(1)} %copy-done.3, bf16[1536,512]{1,0:T(8,128)(2,1)S(1)} %copy-done.1, f32[512,512]{1,0:T(8,128)S(1)} %inverse_factor.1), kind=kOutput, calls=%fused_computation.3 | convolution fusion | flops 1618739200 | bytes 7340032 | tf_op jit(solution)/shard_map/dot_general | solution.py:172
  178.7 2.5 %collective-permute-done.11 = f32[1,512]{1,0:T(1,128)S(1)} collective-permute-done((f32[1,512]{1,0:T(1,128)S(1)}, f32[1,512]{1,0:T(1,128)S(1)}, u32[]{:S(2)}, u32[]{:S(2)}) %collective-permute-start.11) | collective-permute-done | bytes 2080 | tf_op jit(solution)/shard_map/ppermute | solution.py:145
  181.2 2.0 %collective-permute-start.12 = (f32[1,512]{1,0:T(1,128)S(1)}, f32[1,512]{1,0:T(1,128)S(1)}, u32[]{:S(2)}, u32[]{:S(2)}) collective-permute-start(f32[1,512]{1,0:T(1,128)S(1)} %add.96), channel_id=1, source_target_pairs={{0,32},{8,40},{16,48},{24,56},{32,0},{40,8},{48,16},{56,24},{1,33}... | collective-permute-start | bytes 6152 | tf_op jit(solution)/shard_map/ppermute | solution.py:145
  183.2 3.2 %subtract_convert_fusion = bf16[3072,416]{0,1:T(8,128)(2,1)} fusion(bf16[3072,512]{1,0:T(8,128)(2,1)S(1)} %convolution_convert_fusion, f32[416,512]{1,0:T(8,128)S(1)} %get-tuple-element.13, bf16[3072,416]{0,1:T(8,128)(2,1)S(1)} %copy-done.6, bf16[3072,416]{0,1:T(8,128)(2,1)S(1)} %copy-done.8), kind=kOutput, calls=%fused_computation.1 | convolution fusion | flops 1319059456 | bytes 11665408 | tf_op jit(solution)/shard_map/dot_general | solution.py:174
  186.4 2.3 %collective-permute-done.12 = f32[1,512]{1,0:T(1,128)S(1)} collective-permute-done((f32[1,512]{1,0:T(1,128)S(1)}, f32[1,512]{1,0:T(1,128)S(1)}, u32[]{:S(2)}, u32[]{:S(2)}) %collective-permute-start.12) | collective-permute-done | bytes 2080 | tf_op jit(solution)/shard_map/ppermute | solution.py:145
  188.8 3.0 %multiply_convert_fusion = bf16[3072,416]{0,1:T(8,128)(2,1)} fusion(bf16[3072,512]{1,0:T(8,128)(2,1)S(1)} %convolution_convert_fusion, f32[416,512]{1,0:T(8,128)S(1)} %broadcast_divide_fusion), kind=kOutput, calls=%fused_computation | convolution fusion | flops 1311391744 | bytes 6553600 | tf_op jit(solution)/shard_map/dot_general | solution.py:177
  (57 shorter events, 17.0 us)
Async XLA Ops:
  96.8 21.5 %collective-permute-start = (bf16[1536,512]{1,0:T(8,128)(2,1)S(1)}, bf16[1536,512]{1,0:T(8,128)(2,1)}, u32[]{:S(2)}, u32[]{:S(2)}) collective-permute-start(bf16[1536,512]{1,0:T(8,128)(2,1)S(1)} %bitcast.43), channel_id=1, source_target_pairs={{0,1},{1,0},{2,3},{3,2},{4,5},{5,4},{6,7},{7,6},{8,9},{9,8},{10,11... | collective-permute-start | bytes 4718600 | tf_op jit(solution)/shard_map/ppermute | solution.py:123
  98.6 13.9 %all-to-all-start.5 = ((bf16[8,64,512]{2,1,0:T(8,128)(2,1)}), bf16[8,64,512]{2,1,0:T(8,128)(2,1)S(1)}, u32[]{:S(2)}, u32[]{:S(2)}) async-start(bf16[8,64,512]{2,1,0:T(8,128)(2,1)} %bitcast.6), calls=%async_computation.5 | async-start | bytes 1048576 | tf_op jit(solution)/shard_map/all_to_all | solution.py:108
  113.5 14.1 %all-to-all-start.6 = ((bf16[8,64,512]{2,1,0:T(8,128)(2,1)}), bf16[8,64,512]{2,1,0:T(8,128)(2,1)S(1)}, u32[]{:S(2)}, u32[]{:S(2)}) async-start(bf16[8,64,512]{2,1,0:T(8,128)(2,1)} %broadcast_in_dim.25), calls=%async_computation.6 | async-start | bytes 1048576 | tf_op jit(solution)/shard_map/all_to_all | solution.py:108
  118.3 2.2 %copy-start.5 = (bf16[3072,416]{0,1:T(8,128)(2,1)S(1)}, bf16[3072,416]{0,1:T(8,128)(2,1)}, u32[]{:S(2)}) copy-start(bf16[3072,416]{0,1:T(8,128)(2,1)} %param.4) | copy-start | bytes 7667716
  118.3 3.5 %copy-start.7 = (bf16[3072,416]{0,1:T(8,128)(2,1)S(1)}, bf16[3072,416]{0,1:T(8,128)(2,1)}, u32[]{:S(2)}) copy-start(bf16[3072,416]{0,1:T(8,128)(2,1)} %param.3) | copy-start | bytes 7667716
  120.1 3.2 %copy-start = (bf16[1536,512]{1,0:T(8,128)(2,1)}, bf16[1536,512]{1,0:T(8,128)(2,1)S(1)}, u32[]{:S(2)}) copy-start(bf16[1536,512]{1,0:T(8,128)(2,1)S(1)} %get-tuple-element.3) | copy-start | bytes 4718596
  120.1 3.2 %copy-start.2 = (bf16[1536,512]{1,0:T(8,128)(2,1)}, bf16[1536,512]{1,0:T(8,128)(2,1)S(1)}, u32[]{:S(2)}) copy-start(bf16[1536,512]{1,0:T(8,128)(2,1)S(1)} %get-tuple-element.4) | copy-start | bytes 4718596
  123.4 5.1 %collective-permute-start.1 = (bf16[104,512]{1,0:T(8,128)(2,1)S(1)}, bf16[104,512]{1,0:T(8,128)(2,1)S(1)}, u32[]{:S(2)}, u32[]{:S(2)}) collective-permute-start(bf16[104,512]{1,0:T(8,128)(2,1)S(1)} %get-tuple-element.9), channel_id=1, source_target_pairs={{0,64},{64,128},{128,192},{192,0},{1,65},{65,129},{129,193},{193,1... | collective-permute-start | bytes 319496 | tf_op jit(solution)/shard_map/ppermute | solution.py:123
  124.9 5.2 %collective-permute-start.3 = (bf16[104,512]{1,0:T(8,128)(2,1)S(1)}, bf16[104,512]{1,0:T(8,128)(2,1)S(1)}, u32[]{:S(2)}, u32[]{:S(2)}) collective-permute-start(bf16[104,512]{1,0:T(8,128)(2,1)S(1)} %get-tuple-element.10), channel_id=1, source_target_pairs={{0,192},{64,0},{128,64},{192,128},{1,193},{65,1},{129,65},{193,129... | collective-permute-start | bytes 319496 | tf_op jit(solution)/shard_map/ppermute | solution.py:123
  125.5 7.1 %collective-permute-start.2 = (bf16[104,512]{1,0:T(8,128)(2,1)S(1)}, bf16[104,512]{1,0:T(8,128)(2,1)S(1)}, u32[]{:S(2)}, u32[]{:S(2)}) collective-permute-start(bf16[104,512]{1,0:T(8,128)(2,1)S(1)} %get-tuple-element.11), channel_id=1, source_target_pairs={{0,128},{64,192},{128,0},{192,64},{1,129},{65,193},{129,1},{193,65... | collective-permute-start | bytes 319496 | tf_op jit(solution)/shard_map/ppermute | solution.py:123
  132.6 29.8 %collective-permute-start.6 = (bf16[104,512]{1,0:T(8,128)(2,1)S(1)}, bf16[104,512]{1,0:T(8,128)(2,1)S(1)}, u32[]{:S(2)}, u32[]{:S(2)}) collective-permute-start(bf16[104,512]{1,0:T(8,128)(2,1)S(1)} %fusion.18), channel_id=1, source_target_pairs={{0,192},{64,0},{128,64},{192,128},{1,193},{65,1},{129,65},{193,129... | collective-permute-start | bytes 319496 | tf_op jit(solution)/shard_map/ppermute | solution.py:123
  133.6 28.9 %collective-permute-start.5 = (bf16[104,512]{1,0:T(8,128)(2,1)S(1)}, bf16[104,512]{1,0:T(8,128)(2,1)S(1)}, u32[]{:S(2)}, u32[]{:S(2)}) collective-permute-start(bf16[104,512]{1,0:T(8,128)(2,1)S(1)} %fusion.18), channel_id=1, source_target_pairs={{0,128},{64,192},{128,0},{192,64},{1,129},{65,193},{129,1},{193,65... | collective-permute-start | bytes 319496 | tf_op jit(solution)/shard_map/ppermute | solution.py:123
  134.8 27.7 %collective-permute-start.4 = (bf16[104,512]{1,0:T(8,128)(2,1)S(1)}, bf16[104,512]{1,0:T(8,128)(2,1)S(1)}, u32[]{:S(2)}, u32[]{:S(2)}) collective-permute-start(bf16[104,512]{1,0:T(8,128)(2,1)S(1)} %fusion.18), channel_id=1, source_target_pairs={{0,64},{64,128},{128,192},{192,0},{1,65},{65,129},{129,193},{193,1... | collective-permute-start | bytes 319496 | tf_op jit(solution)/shard_map/ppermute | solution.py:123
  162.4 14.3 %copy-start.1 = (bf16[1536,512]{1,0:T(8,128)(2,1)S(1)}, bf16[1536,512]{1,0:T(8,128)(2,1)}, u32[]{:S(2)}) copy-start(bf16[1536,512]{1,0:T(8,128)(2,1)} %copy-done) | copy-start | bytes 4718596
  162.5 14.3 %copy-start.3 = (bf16[1536,512]{1,0:T(8,128)(2,1)S(1)}, bf16[1536,512]{1,0:T(8,128)(2,1)}, u32[]{:S(2)}) copy-start(bf16[1536,512]{1,0:T(8,128)(2,1)} %copy-done.2) | copy-start | bytes 4718596
  163.1 1.2 collective-permute-start.7
  164.3 3.6 %collective-permute-start.8 = (f32[1,512]{1,0:T(1,128)S(1)}, f32[1,512]{1,0:T(1,128)S(1)}, u32[]{:S(2)}, u32[]{:S(2)}) collective-permute-start(f32[1,512]{1,0:T(1,128)S(1)} %add.92), channel_id=1, source_target_pairs={{0,2},{2,0},{4,6},{6,4},{1,3},{3,1},{5,7},{7,5},{8,10},{10,8},{12,... | collective-permute-start | bytes 6152 | tf_op jit(solution)/shard_map/ppermute | solution.py:145
  167.9 5.1 %collective-permute-start.9 = (f32[1,512]{1,0:T(1,128)S(1)}, f32[1,512]{1,0:T(1,128)S(1)}, u32[]{:S(2)}, u32[]{:S(2)}) collective-permute-start(f32[1,512]{1,0:T(1,128)S(1)} %add.93), channel_id=1, source_target_pairs={{0,4},{2,6},{4,0},{6,2},{1,5},{3,7},{5,1},{7,3},{8,12},{10,14},{12... | collective-permute-start | bytes 6152 | tf_op jit(solution)/shard_map/ppermute | solution.py:145
  173.0 3.6 %collective-permute-start.10 = (f32[1,512]{1,0:T(1,128)S(1)}, f32[1,512]{1,0:T(1,128)S(1)}, u32[]{:S(2)}, u32[]{:S(2)}) collective-permute-start(f32[1,512]{1,0:T(1,128)S(1)} %add.94), channel_id=1, source_target_pairs={{0,8},{8,0},{16,24},{24,16},{32,40},{40,32},{48,56},{56,48},{1,9},... | collective-permute-start | bytes 6152 | tf_op jit(solution)/shard_map/ppermute | solution.py:145
  176.6 6.6 %copy-start.6 = (bf16[3072,416]{0,1:T(8,128)(2,1)S(1)}, bf16[3072,416]{0,1:T(8,128)(2,1)}, u32[]{:S(2)}) copy-start(bf16[3072,416]{0,1:T(8,128)(2,1)} %param.4) | copy-start | bytes 7667716
  176.6 6.6 %copy-start.8 = (bf16[3072,416]{0,1:T(8,128)(2,1)S(1)}, bf16[3072,416]{0,1:T(8,128)(2,1)}, u32[]{:S(2)}) copy-start(bf16[3072,416]{0,1:T(8,128)(2,1)} %param.3) | copy-start | bytes 7667716
  176.6 4.6 %collective-permute-start.11 = (f32[1,512]{1,0:T(1,128)S(1)}, f32[1,512]{1,0:T(1,128)S(1)}, u32[]{:S(2)}, u32[]{:S(2)}) collective-permute-start(f32[1,512]{1,0:T(1,128)S(1)} %add.95), channel_id=1, source_target_pairs={{0,16},{8,24},{16,0},{24,8},{32,48},{40,56},{48,32},{56,40},{1,17}... | collective-permute-start | bytes 6152 | tf_op jit(solution)/shard_map/ppermute | solution.py:145
  181.2 7.5 %collective-permute-start.12 = (f32[1,512]{1,0:T(1,128)S(1)}, f32[1,512]{1,0:T(1,128)S(1)}, u32[]{:S(2)}, u32[]{:S(2)}) collective-permute-start(f32[1,512]{1,0:T(1,128)S(1)} %add.96), channel_id=1, source_target_pairs={{0,32},{8,40},{16,48},{24,56},{32,0},{40,8},{48,16},{56,24},{1,33}... | collective-permute-start | bytes 6152 | tf_op jit(solution)/shard_map/ppermute | solution.py:145
  188.8 3.0 %copy-start.4 = (f32[416,512]{1,0:T(8,128)}, f32[416,512]{1,0:T(8,128)S(1)}, u32[]{:S(2)}) copy-start(f32[416,512]{1,0:T(8,128)S(1)} %broadcast_divide_fusion) | copy-start | bytes 2555908

commit v2 on v0

v2 whole, which is shorter than its diff:
```python
import math

import jax
import jax.numpy as jnp
from jax import lax
from jax.experimental import pallas as pl
from jax.experimental.pallas import tpu as pltpu
from jax.sharding import Mesh
from jax.sharding import PartitionSpec as P

RANK = 512
NB = 128
F32 = jnp.float32
BF16 = jnp.bfloat16
error_share = 0.05
epsilon = 1e-06


def split(value):
    high = value.astype(BF16)
    return high, (value - high.astype(F32)).astype(BF16)


def product3(left, right, dims):
    left_high, left_low = split(left)
    right_high, right_low = split(right)
    dot = lambda a, b: lax.dot_general(a, b, dims, preferred_element_type=F32)
    return dot(left_high, right_high) + (dot(left_high, right_low) + dot(left_low, right_high))


def factor_block(w_ref, sub, lane):
    groups = NB // 8
    wide = (8, NB)
    row_of = lambda value, k: jnp.broadcast_to(value[k : k + 1, :], wide)
    columns = lambda value, at: [jnp.broadcast_to(value[:, at + j : at + j + 1], wide) for j in range(8)]
    for b in range(groups):
        r0 = 8 * b
        mine = (lane >= r0) & (lane < r0 + 8)
        more = b + 1 < groups
        top = w_ref[r0 : r0 + 8, :]
        cols = columns(top, r0)
        top = jnp.where(mine, jnp.where(lane - r0 == sub, 1.0, 0.0), top)
        if more:
            below = w_ref[r0 + 8 : r0 + 16, :]
            next_cols = columns(below, r0)
            below = jnp.where(mine, 0.0, below)
        pivots = jnp.ones(wide, F32)
        rows, inverse, coef = [], [], {}
        for k in range(8):
            pivot = row_of(cols[k], k)
            recip = 1.0 / pivot
            pivots = jnp.where(sub == k, pivot, pivots)
            row = row_of(top, k)
            factor = jnp.where(sub > k, cols[k] * recip, 0.0)
            if more:
                next_factor = next_cols[k] * recip
            for j in range(k + 1, 8):
                coef[k, j] = row_of(cols[j], k)
                cols[j] = cols[j] - factor * coef[k, j]
                if more:
                    next_cols[j] = next_cols[j] - next_factor * coef[k, j]
            top = top - factor * row
            if more:
                below = below - next_factor * row
            rows.append(row)
            inverse.append(recip)
        w_ref[r0 : r0 + 8, :] = top * lax.rsqrt(pivots)
        if more:
            w_ref[r0 + 8 : r0 + 16, :] = below
        for v in range(b + 2, groups):
            q = 8 * v
            low = w_ref[q : q + 8, :]
            lead = columns(low, r0)
            low = jnp.where(mine, 0.0, low)
            for k in range(8):
                factor = lead[k] * inverse[k]
                for j in range(k + 1, 8):
                    lead[j] = lead[j] - factor * coef[k, j]
                low = low - factor * rows[k]
            w_ref[q : q + 8, :] = low


def chol_kernel(pos_ref, mine_ref, other_ref, half_ref, o_ref, w_ref):
    sub = lax.broadcasted_iota(jnp.int32, (8, NB), 0)
    lane = lax.broadcasted_iota(jnp.int32, (8, NB), 1)
    lower = lax.broadcasted_iota(jnp.int32, (NB, NB), 0) >= lax.broadcasted_iota(jnp.int32, (NB, NB), 1)
    wide_lane = lax.broadcasted_iota(jnp.int32, (NB, RANK), 1)
    tall_row = lax.broadcasted_iota(jnp.int32, (RANK, NB), 0)
    pieces = 4
    tall = mine_ref.shape[0] // pieces
    for j in range(pieces):
        at = ((pos_ref[2] - j) & (pieces - 1)) * tall
        here = slice(j * tall, (j + 1) * tall)
        o_ref[pl.ds(pl.multiple_of(at + pos_ref[0] * (RANK // 2), tall), tall), :] = mine_ref[here, :].astype(F32)
        o_ref[pl.ds(pl.multiple_of(at + (1 - pos_ref[0]) * (RANK // 2), tall), tall), :] = other_ref[here, :].astype(F32)

    def step(p, carry):
        at = pl.multiple_of(p * NB, NB)
        here = pl.ds(at, NB)
        w_ref[...] = o_ref[here, here]
        factor_block(w_ref, sub, lane)
        block = jnp.where(lower, w_ref[...], 0.0)
        panel = product3(block, o_ref[here, :], (((1,), (0,)), ((), ())))
        o_ref[here, :] = panel
        o_ref[here, here] = block
        rest = jnp.where(wide_lane >= at + NB, panel, 0.0)
        o_ref[:, here] = jnp.where(tall_row >= at + NB, 0.0, o_ref[:, here])
        o_ref[...] -= product3(rest, o_ref[here, :], (((0,), (0,)), ((), ())))
        return carry

    lax.fori_loop(0, RANK // NB, step, 0)
    row = lax.broadcasted_iota(jnp.int32, (RANK, RANK), 0)
    col = lax.broadcasted_iota(jnp.int32, (RANK, RANK), 1)
    half_ref[...] = jnp.where(row >= col, o_ref[...], 0.0).astype(BF16)


SMEM = pl.BlockSpec(memory_space=pltpu.SMEM)
VMEM = pl.BlockSpec(memory_space=pltpu.VMEM)


def local(kernel, name, ins, outs, flops, scratch=()):
    shapes = [jax.ShapeDtypeStruct(shape, dtype) for shape, dtype in outs]
    moved = sum(v.size * v.dtype.itemsize for v in (*ins, *shapes))
    return pl.pallas_call(
        kernel,
        out_shape=shapes,
        in_specs=[SMEM] + [VMEM] * (len(ins) - 1),
        out_specs=[VMEM] * len(outs),
        scratch_shapes=[pltpu.VMEM(shape, dtype) for shape, dtype in scratch],
        compiler_params=pltpu.CompilerParams(vmem_limit_bytes=6 * 1024 * 1024),
        cost_estimate=pl.CostEstimate(flops=flops, bytes_accessed=moved, transcendentals=0),
        name=name,
    )(*ins)


def inverse_factor(pos, mine, other):
    square = (RANK, RANK)
    return local(
        chol_kernel,
        "inverse_factor",
        (pos, mine, other),
        [(square, BF16)],
        20_000_000_000,
        [(square, F32), ((NB, NB), F32)],
    )[0]


def swap(pieces, axis):
    return lax.all_to_all(pieces, axis, 0, 0, tiled=True)


def scatter_swap(block, axis, n):
    got = swap(block.reshape(n, block.shape[0] // n, RANK), axis)
    return jnp.sum(got.astype(F32), axis=0).astype(BF16)


def gather_swap(block, axis, n):
    got = swap(jnp.broadcast_to(block[None], (n, *block.shape)), axis)
    return got.reshape(n * block.shape[0], RANK)


def shift(value, axis, n, by):
    return lax.ppermute(value, axis, [(i, (i + by) % n) for i in range(n)])


def piece(block, i, n):
    rows = block.shape[0] // n
    return lax.dynamic_slice_in_dim(block, (i & (n - 1)) * rows, rows, 0)


def scatter_shift(block, axis, n):
    me = lax.axis_index(axis)
    got = [shift(piece(block, me + by, n), axis, n, by) for by in range(1, n)]
    return sum((g.astype(F32) for g in got), piece(block, me, n).astype(F32)).astype(BF16)


def gather_shift(block, axis, n):
    return [block] + [shift(block, axis, n, by) for by in range(1, n)]


def in_order(blocks, axis):
    n = len(blocks)
    me = lax.axis_index(axis)
    held = jnp.concatenate(blocks)
    return jnp.concatenate([piece(held, me - i + n, n) for i in range(n)])


def add(*values):
    return sum(v.astype(F32) for v in values)


def add_four(v):
    own, one, two, three = (x.astype(F32) for x in v)
    return (own + two) + (one + three)


def trade(value):
    return shift(value, "core", 2, 1)


def all_sum(value, sizes):
    value = value + trade(value)
    value = add_four(gather_shift(value, "x", sizes["x"]))
    for step in (1, 2, 4):
        value = value + lax.ppermute(value, "z", [(i, i ^ step) for i in range(sizes["z"])])
    return value


TN = (((0,), (0,)), ((), ()))
NN = (((1,), (0,)), ((), ()))
NT = (((1,), (1,)), ((), ()))


def dot(a, b, dims):
    return lax.dot_general(a, b, dims, preferred_element_type=F32)


def shards(sizes, whole, momentum, gradient, right_basis):
    nx, nz, ny = sizes["x"], sizes["z"], sizes["row"]
    pos = jnp.stack([lax.axis_index(axis) for axis in ("core", "x", "row")]).astype(jnp.int32)
    core = lax.axis_index("core")
    low = core == 0
    half = momentum.shape[0] // 2
    cut = half * 2 // 3
    basis_half = right_basis.astype(BF16)

    def part_of(which):
        mom = lax.dynamic_slice_in_dim(momentum, which * half, half, 0)
        grad = lax.dynamic_slice_in_dim(gradient, which * half, half, 0)
        return dot((mom.astype(F32) + grad.astype(F32)).astype(BF16), basis_half, NN)

    away = part_of(1 - core).astype(BF16)
    got = jnp.concatenate([trade(away[: half // 2]), trade(away[half // 2 :])])
    part = (part_of(core) + got.astype(F32)).astype(BF16)
    first, second = part[:cut], part[cut:]
    first = scatter_shift(first, "x", nx)
    second = scatter_swap(second, "z", nz)
    second = scatter_shift(second, "x", nx)
    first = scatter_swap(first, "z", nz)
    first = gather_swap(first, "z", nz)
    second = in_order(gather_shift(second, "x", nx), "x")
    first = gather_shift(first, "x", nx)
    second = gather_swap(second, "z", nz)

    held = jnp.concatenate(first)
    gram_part = (dot(held, held, TN) + dot(second, second, TN)).astype(BF16)
    gram = add(piece(gram_part, core, 2), trade(piece(gram_part, 1 - core, 2))).astype(BF16)
    mine = jnp.concatenate([in_order(first, "x"), second])
    other = trade(mine)
    gram = scatter_shift(gram, "row", ny)
    gram = jnp.concatenate(gather_shift(gram, "row", ny))
    blended = (momentum.astype(F32) + gradient.astype(F32)).astype(BF16)
    projected = jnp.concatenate([jnp.where(low, mine, other), jnp.where(low, other, mine)])
    cross = dot(blended, projected, TN).astype(BF16)
    gram, cross = lax.optimization_barrier((gram, cross))
    cross = gather_shift(cross, "row", ny)
    inverse = inverse_factor(pos, gram, trade(gram))
    back_proj = dot(add_four(cross).astype(BF16), inverse, NT)
    col_sq = all_sum(jnp.sum(back_proj * back_proj, axis=0, keepdims=True), sizes)
    ortho_half = dot(projected, inverse, NT).astype(BF16)
    low_rank = dot(ortho_half, back_proj.astype(BF16), NT)
    new_momentum = (blended.astype(F32) - error_share * low_rank).astype(BF16)
    new_basis = back_proj / (jnp.sqrt(col_sq) + epsilon)
    product = dot(ortho_half, new_basis.astype(BF16), NT)
    direction = (product * math.sqrt(whole / RANK)).astype(BF16)
    return (new_momentum, new_basis, direction)


def solution(mesh):
    sizes = {"row": 4, "z": 8, "x": 4, "core": 2}
    inner = Mesh(mesh.devices.reshape(tuple(sizes.values())), tuple(sizes))
    col = ("z", "x", "core")

    def step(momentum, gradient, right_basis):
        whole = momentum.shape[0] * momentum.shape[1]
        body = lambda *args: shards(sizes, whole, *args)
        return jax.shard_map(
            body,
            mesh=inner,
            in_specs=(P("row", col), P("row", col), P(col, None)),
            out_specs=(P("row", col), P(col, None), P("row", col)),
            check_vma=False,
        )(momentum, gradient, right_basis)

    return step
```

time: 640 us -> 166 us (0.26)
  waiting for transfers between devices: 297 us -> 55.4 us
  blocking collectives: 127 us -> 0 us
  other arithmetic: 122 us -> 3.17 us
  starting transfers between devices: 0.3 us -> 63.8 us
  matrix products: 61.9 us -> 17.2 us
  Pallas kernels: 0 us -> 20.4 us
  between operations: 16.9 us -> 1 us
    psum x3 -> x0, waiting for transfers between devices: 297 us -> none  [the longest x1 203 us: shards(): projected = lax.psum(partial_proj, 'col')]
    psum x1 -> x0, blocking collectives: 127 us -> none  [shards(): col_sq = lax.psum(jnp.sum(back_proj * back_proj, axis=0), 'col')]
    another operation x17 -> x1, other arithmetic: 118 us -> 0.08 us  [shards(): jnp.stack([lax.axis_index(axis) for axis in ('core', 'x', 'row')])]
    ppermute x0 -> x33, waiting for transfers between devices: none -> 43.7 us  [the longest x30 39.3 us: shift(): return lax.ppermute(value, axis, [(i, (i + by) % n) for i in range(n)])]
    ppermute x0 -> x33, starting transfers between devices: none -> 41 us  [the longest x30 34.6 us: shift(): return lax.ppermute(value, axis, [(i, (i + by) % n) for i in range(n)])]
    another operation x13 -> x0, matrix products: 29.8 us -> none  [the longest x7 27.9 us: orthonormalize(): lax.linalg.triangular_solve(chol_factor, block, left_side=False, lower=Tr...]
    all_to_all x0 -> x4, starting transfers between devices: none -> 22.8 us  [swap(): return lax.all_to_all(pieces, axis, 0, 0, tiled=True)]
    pallas_call x0 -> x1, Pallas kernels: none -> 20.4 us  [local(): pl.pallas_call(kernel, out_shape=shapes, in_specs=[SMEM] + [VMEM] * (len(...]
  transfers between devices with their start and end apart: 3 -> 37, of which waited for: 3 -> 24; matrix products, arithmetic and copies ran while one was open for 0% -> 5% of each run, Pallas kernels for 0% -> 12%
where the time goes in v2:
time: 166 us; the launch traced here: 165 us
  starting transfers between devices  63.8 us (38%)
  waiting for transfers between devices  55.4 us (33%)
  Pallas kernels  20.4 us (12%)
  matrix products  17.2 us (10%)
  local copies, waits for them, and re-layouts  4.52 us (3%)
  other arithmetic  3.17 us (2%)
    ppermute x30, waiting for transfers between devices, shift(): return lax.ppermute(value, axis, [(i, (i + by) % n) for i in range(n)])  39.3 us
    ppermute x30, starting transfers between devices, shift(): return lax.ppermute(value, axis, [(i, (i + by) % n) for i in range(n)])  34.6 us
    all_to_all x4, starting transfers between devices, swap(): return lax.all_to_all(pieces, axis, 0, 0, tiled=True)  22.8 us
    pallas_call x1, Pallas kernels, local(): pl.pallas_call(kernel, out_shape=shapes, in_specs=[SMEM] + [VMEM] * (len(...  20.4 us
    dot_general x9, matrix products, dot(): return lax.dot_general(a, b, dims, preferred_element_type=F32)  17.2 us
    all_to_all x4, waiting for transfers between devices, swap(): return lax.all_to_all(pieces, axis, 0, 0, tiled=True)  11.7 us
    ppermute x3, starting transfers between devices, all_sum(): lax.ppermute(value, 'z', [(i, i ^ step) for i in range(sizes['z'])])  6.37 us
    ppermute x3, waiting for transfers between devices, all_sum(): lax.ppermute(value, 'z', [(i, i ^ step) for i in range(sizes['z'])])  4.38 us
  transfers between devices with their start and end apart: 37, of which 24 were waited for; matrix products, arithmetic and copies ran while one was open for 5% of the time, Pallas kernels for 12%

profile of v2, /device:TPU:8, one launch (start us, length us, event | category | flops | bytes accessed | tf_op | source)
XLA Modules:
  0.0 165.4 jit_solution(2603145749298279091)
XLA Ops:
  0.6 3.0 %convolution_convert_fusion.1 = bf16[1536,512]{1,0:T(8,128)(2,1)S(1)} fusion(bf16[3072,416]{0,1:T(8,128)(2,1)} %param.4, s32[]{:T(128)S(6)} %select_n.76, bf16[3072,416]{0,1:T(8,128)(2,1)} %param.3, f32[416,512]{1,0:T(8,128)} %param.5), kind=kOutput, calls=%fused_computation.6 | convolution fusion | flops 657866752 | bytes 4980740 | tf_op jit(solution)/shard_map/dot_general | solution.py:215
  7.4 3.2 %add_convert_fusion.1 = bf16[1536,512]{1,0:T(8,128)(2,1)S(1)} fusion(bf16[768,512]{1,0:T(8,128)(2,1)} %collective-permute-done.1, bf16[768,512]{1,0:T(8,128)(2,1)} %collective-permute-done, bf16[3072,416]{0,1:T(8,128)(2,1)} %param.4, s32[]{:T(128)S(6)} %select_n.75, bf16[3072,416]{0,1:T(8,128)(2,1)} %param.3, f32[416,512]{1,0:T(8,128)S(1)} %copy-done.5), kind=kOutput, calls=%fused_computation.5 | convolution fusion | flops 661798912 | bytes 6553604 | tf_op jit(solution)/shard_map/dot_general | solution.py:215
  11.4 8.5 %all-to-all-start.2 = ((bf16[8,64,512]{2,1,0:T(8,128)(2,1)}), bf16[8,64,512]{2,1,0:T(8,128)(2,1)S(1)}, u32[]{:S(2)}, u32[]{:S(2)}) async-start(bf16[8,64,512]{2,1,0:T(8,128)(2,1)} %bitcast.2), calls=%async_computation.2 | async-start | bytes 1048576 | tf_op jit(solution)/shard_map/all_to_all | solution.py:149
  25.1 4.4 %collective-permute-done.2 = bf16[256,512]{1,0:T(8,128)(2,1)S(1)} collective-permute-done((bf16[256,512]{1,0:T(8,128)(2,1)S(1)}, bf16[256,512]{1,0:T(8,128)(2,1)S(1)}, u32[]{:S(2)}, u32[]{:S(2)}) %collective-permute-start.2) | collective-permute-done | bytes 262176 | tf_op jit(solution)/shard_map/ppermute | solution.py:163
  29.5 4.8 %collective-permute-done.4 = bf16[256,512]{1,0:T(8,128)(2,1)S(1)} collective-permute-done((bf16[256,512]{1,0:T(8,128)(2,1)S(1)}, bf16[256,512]{1,0:T(8,128)(2,1)S(1)}, u32[]{:S(2)}, u32[]{:S(2)}) %collective-permute-start.4) | collective-permute-done | bytes 262176 | tf_op jit(solution)/shard_map/ppermute | solution.py:163
  37.6 6.1 %all-to-all-start = ((bf16[8,32,512]{2,1,0:T(8,128)(2,1)}), bf16[8,32,512]{2,1,0:T(8,128)(2,1)S(1)}, u32[]{:S(2)}, u32[]{:S(2)}) async-start(bf16[8,32,512]{2,1,0:T(8,128)(2,1)} %bitcast), calls=%async_computation | async-start | bytes 524288 | tf_op jit(solution)/shard_map/all_to_all | solution.py:149
  45.0 2.1 %collective-permute-start.10 = (bf16[16,512]{1,0:T(8,128)(2,1)S(1)}, bf16[16,512]{1,0:T(8,128)(2,1)S(1)}, u32[]{:S(2)}, u32[]{:S(2)}) collective-permute-start(bf16[16,512]{1,0:T(8,128)(2,1)S(1)} %get-tuple-element.22), channel_id=1, source_target_pairs={{0,6},{2,0},{4,2},{6,4},{1,7},{3,1},{5,3},{7,5},{8,14},{10,8},{12,... | collective-permute-start | bytes 49160 | tf_op jit(solution)/shard_map/ppermute | solution.py:163
  47.3 7.1 %all-to-all-done = bf16[8,32,512]{2,1,0:T(8,128)(2,1)S(1)} async-done(((bf16[8,32,512]{2,1,0:T(8,128)(2,1)}), bf16[8,32,512]{2,1,0:T(8,128)(2,1)S(1)}, u32[]{:S(2)}, u32[]{:S(2)}) %all-to-all-start) | async-done | bytes 262176 | tf_op jit(solution)/shard_map/all_to_all | solution.py:149
  55.2 3.4 %all-to-all-start.1 = ((bf16[8,32,512]{2,1,0:T(8,128)(2,1)}), bf16[8,32,512]{2,1,0:T(8,128)(2,1)S(1)}, u32[]{:S(2)}, u32[]{:S(2)}) async-start(bf16[8,32,512]{2,1,0:T(8,128)(2,1)} %broadcast_in_dim.6), calls=%async_computation.1 | async-start | bytes 524288 | tf_op jit(solution)/shard_map/all_to_all | solution.py:149
  62.5 3.3 %collective-permute-done.12 = bf16[16,512]{1,0:T(8,128)(2,1)S(1)} collective-permute-done((bf16[16,512]{1,0:T(8,128)(2,1)S(1)}, bf16[16,512]{1,0:T(8,128)(2,1)S(1)}, u32[]{:S(2)}, u32[]{:S(2)}) %collective-permute-start.12) | collective-permute-done | bytes 16416 | tf_op jit(solution)/shard_map/ppermute | solution.py:163
  66.7 2.3 %all-to-all-done.1 = bf16[8,32,512]{2,1,0:T(8,128)(2,1)S(1)} async-done(((bf16[8,32,512]{2,1,0:T(8,128)(2,1)}), bf16[8,32,512]{2,1,0:T(8,128)(2,1)S(1)}, u32[]{:S(2)}, u32[]{:S(2)}) %all-to-all-start.1) | async-done | bytes 262176 | tf_op jit(solution)/shard_map/all_to_all | solution.py:149
  69.8 4.8 %all-to-all-start.3 = ((bf16[8,64,512]{2,1,0:T(8,128)(2,1)}), bf16[8,64,512]{2,1,0:T(8,128)(2,1)S(1)}, u32[]{:S(2)}, u32[]{:S(2)}) async-start(bf16[8,64,512]{2,1,0:T(8,128)(2,1)} %broadcast_in_dim.7), calls=%async_computation.3 | async-start | bytes 1048576 | tf_op jit(solution)/shard_map/all_to_all | solution.py:149
  77.2 3.9 %collective-permute-done.7 = bf16[256,512]{1,0:T(8,128)(2,1)S(1)} collective-permute-done((bf16[256,512]{1,0:T(8,128)(2,1)S(1)}, bf16[256,512]{1,0:T(8,128)(2,1)S(1)}, u32[]{:S(2)}, u32[]{:S(2)}) %collective-permute-start.7) | collective-permute-done | bytes 262176 | tf_op jit(solution)/shard_map/ppermute | solution.py:163
  81.0 2.5 %collective-permute-done.6 = bf16[256,512]{1,0:T(8,128)(2,1)S(1)} collective-permute-done((bf16[256,512]{1,0:T(8,128)(2,1)S(1)}, bf16[256,512]{1,0:T(8,128)(2,1)S(1)}, u32[]{:S(2)}, u32[]{:S(2)}) %collective-permute-start.6) | collective-permute-done | bytes 262176 | tf_op jit(solution)/shard_map/ppermute | solution.py:163
  83.5 2.7 %collective-permute-done.5 = bf16[256,512]{1,0:T(8,128)(2,1)S(1)} collective-permute-done((bf16[256,512]{1,0:T(8,128)(2,1)S(1)}, bf16[256,512]{1,0:T(8,128)(2,1)S(1)}, u32[]{:S(2)}, u32[]{:S(2)}) %collective-permute-start.5) | collective-permute-done | bytes 262176 | tf_op jit(solution)/shard_map/ppermute | solution.py:163
  94.1 2.3 %collective-permute-start.17 = (bf16[64,512]{1,0:T(8,128)(2,1)S(1)}, bf16[64,512]{1,0:T(8,128)(2,1)S(1)}, u32[]{:S(2)}, u32[]{:S(2)}) collective-permute-start(bf16[64,512]{1,0:T(8,128)(2,1)S(1)} %get-tuple-element.16), channel_id=1, source_target_pairs={{0,128},{64,192},{128,0},{192,64},{1,129},{65,193},{129,1},{193,65... | collective-permute-start | bytes 196616 | tf_op jit(solution)/shard_map/ppermute | solution.py:163
  104.9 2.5 %collective-permute-done.20 = bf16[64,512]{1,0:T(8,128)(2,1)S(1)} collective-permute-done((bf16[64,512]{1,0:T(8,128)(2,1)S(1)}, bf16[64,512]{1,0:T(8,128)(2,1)S(1)}, u32[]{:S(2)}, u32[]{:S(2)}) %collective-permute-start.20) | collective-permute-done | bytes 65568 | tf_op jit(solution)/shard_map/ppermute | solution.py:163
  112.1 2.5 %collective-permute-start.25 = (bf16[416,512]{1,0:T(8,128)(2,1)S(1)}, bf16[416,512]{1,0:T(8,128)(2,1)S(1)}, u32[]{:S(2)}, u32[]{:S(2)}) collective-permute-start(bf16[416,512]{1,0:T(8,128)(2,1)S(1)} %fusion.7), channel_id=1, source_target_pairs={{0,192},{64,0},{128,64},{192,128},{1,193},{65,1},{129,65},{193,129... | collective-permute-start | bytes 1277960 | tf_op jit(solution)/shard_map/ppermute | solution.py:163
  114.6 2.8 %collective-permute-start.23 = (bf16[416,512]{1,0:T(8,128)(2,1)S(1)}, bf16[416,512]{1,0:T(8,128)(2,1)S(1)}, u32[]{:S(2)}, u32[]{:S(2)}) collective-permute-start(bf16[416,512]{1,0:T(8,128)(2,1)S(1)} %fusion.7), channel_id=1, source_target_pairs={{0,128},{64,192},{128,0},{192,64},{1,129},{65,193},{129,1},{193,65... | collective-permute-start | bytes 1277960 | tf_op jit(solution)/shard_map/ppermute | solution.py:163
  117.4 20.4 %inverse_factor.1 = bf16[512,512]{1,0:T(8,128)(2,1)S(1)} custom-call(s32[3]{0:T(128)S(1)} %pad_add_fusion.pos_ref, bf16[256,512]{1,0:T(8,128)(2,1)S(1)} %pad_maximum_fusion.6.mine_ref, bf16[256,512]{1,0:T(8,128)(2,1)S(1)} %collective-permute-done.22.other_ref), custom_call_target="tpu_custom_call" | custom-call | flops 20000000000 | bytes 1048588 | tf_op jit(solution)/shard_map/inverse_factor/pallas_call | solution.py:124
  147.2 3.1 %collective-permute-done.30 = f32[1,512]{1,0:T(1,128)S(1)} collective-permute-done((f32[1,512]{1,0:T(1,128)S(1)}, f32[1,512]{1,0:T(1,128)S(1)}, u32[]{:S(2)}, u32[]{:S(2)}) %collective-permute-start.30) | collective-permute-done | bytes 2080 | tf_op jit(solution)/shard_map/ppermute | solution.py:205
  154.8 4.4 %collective-permute-start.32 = (f32[1,512]{1,0:T(1,128)S(1)}, f32[1,512]{1,0:T(1,128)S(1)}, u32[]{:S(2)}, u32[]{:S(2)}) collective-permute-start(f32[1,512]{1,0:T(1,128)S(1)} %add.231), channel_id=1, source_target_pairs={{0,32},{8,40},{16,48},{24,56},{32,0},{40,8},{48,16},{56,24},{1,33}... | collective-permute-start | bytes 6152 | tf_op jit(solution)/shard_map/ppermute | solution.py:205
  159.2 3.1 %subtract_convert_fusion = bf16[3072,416]{0,1:T(8,128)(2,1)} fusion(bf16[3072,512]{1,0:T(8,128)(2,1)S(1)} %convolution_convert_fusion, bf16[3072,416]{0,1:T(8,128)(2,1)S(1)} %copy-done.3, bf16[3072,416]{0,1:T(8,128)(2,1)S(1)} %copy-done.4, f32[416,512]{1,0:T(8,128)S(1)} %get-tuple-element.25), kind=kOutput, calls=%fused_computation.1 | convolution fusion | flops 1319059456 | bytes 11665408 | tf_op jit(solution)/shard_map/dot_general | solution.py:215
  162.4 3.0 %multiply_convert_fusion = bf16[3072,416]{0,1:T(8,128)(2,1)} fusion(bf16[3072,512]{1,0:T(8,128)(2,1)S(1)} %convolution_convert_fusion, f32[416,512]{1,0:T(8,128)S(1)} %broadcast_divide_fusion), kind=kOutput, calls=%fused_computation | convolution fusion | flops 1311391744 | bytes 6553600 | tf_op jit(solution)/shard_map/dot_general | solution.py:215
  (105 shorter events, 58.6 us)
Async XLA Ops:
  11.4 26.3 %all-to-all-start.2 = ((bf16[8,64,512]{2,1,0:T(8,128)(2,1)}), bf16[8,64,512]{2,1,0:T(8,128)(2,1)S(1)}, u32[]{:S(2)}, u32[]{:S(2)}) async-start(bf16[8,64,512]{2,1,0:T(8,128)(2,1)} %bitcast.2), calls=%async_computation.2 | async-start | bytes 1048576 | tf_op jit(solution)/shard_map/all_to_all | solution.py:149
  20.0 9.5 %collective-permute-start.2 = (bf16[256,512]{1,0:T(8,128)(2,1)S(1)}, bf16[256,512]{1,0:T(8,128)(2,1)S(1)}, u32[]{:S(2)}, u32[]{:S(2)}) collective-permute-start(bf16[256,512]{1,0:T(8,128)(2,1)S(1)} %get-tuple-element.11), channel_id=1, source_target_pairs={{0,2},{2,4},{4,6},{6,0},{1,3},{3,5},{5,7},{7,1},{8,10},{10,12},{12... | collective-permute-start | bytes 786440 | tf_op jit(solution)/shard_map/ppermute | solution.py:163
  21.5 12.7 %collective-permute-start.4 = (bf16[256,512]{1,0:T(8,128)(2,1)S(1)}, bf16[256,512]{1,0:T(8,128)(2,1)S(1)}, u32[]{:S(2)}, u32[]{:S(2)}) collective-permute-start(bf16[256,512]{1,0:T(8,128)(2,1)S(1)} %get-tuple-element.12), channel_id=1, source_target_pairs={{0,6},{2,0},{4,2},{6,4},{1,7},{3,1},{5,3},{7,5},{8,14},{10,8},{12,... | collective-permute-start | bytes 786440 | tf_op jit(solution)/shard_map/ppermute | solution.py:163
  23.3 12.6 %collective-permute-start.3 = (bf16[256,512]{1,0:T(8,128)(2,1)S(1)}, bf16[256,512]{1,0:T(8,128)(2,1)S(1)}, u32[]{:S(2)}, u32[]{:S(2)}) collective-permute-start(bf16[256,512]{1,0:T(8,128)(2,1)S(1)} %get-tuple-element.13), channel_id=1, source_target_pairs={{0,4},{2,6},{4,0},{6,2},{1,5},{3,7},{5,1},{7,3},{8,12},{10,14},{12... | collective-permute-start | bytes 786440 | tf_op jit(solution)/shard_map/ppermute | solution.py:163
  37.6 16.8 %all-to-all-start = ((bf16[8,32,512]{2,1,0:T(8,128)(2,1)}), bf16[8,32,512]{2,1,0:T(8,128)(2,1)S(1)}, u32[]{:S(2)}, u32[]{:S(2)}) async-start(bf16[8,32,512]{2,1,0:T(8,128)(2,1)} %bitcast), calls=%async_computation | async-start | bytes 524288 | tf_op jit(solution)/shard_map/all_to_all | solution.py:149
  43.8 14.8 %collective-permute-start.8 = (bf16[16,512]{1,0:T(8,128)(2,1)S(1)}, bf16[16,512]{1,0:T(8,128)(2,1)S(1)}, u32[]{:S(2)}, u32[]{:S(2)}) collective-permute-start(bf16[16,512]{1,0:T(8,128)(2,1)S(1)} %get-tuple-element.21), channel_id=1, source_target_pairs={{0,2},{2,4},{4,6},{6,0},{1,3},{3,5},{5,7},{7,1},{8,10},{10,12},{12... | collective-permute-start | bytes 49160 | tf_op jit(solution)/shard_map/ppermute | solution.py:163
  45.0 13.6 %collective-permute-start.10 = (bf16[16,512]{1,0:T(8,128)(2,1)S(1)}, bf16[16,512]{1,0:T(8,128)(2,1)S(1)}, u32[]{:S(2)}, u32[]{:S(2)}) collective-permute-start(bf16[16,512]{1,0:T(8,128)(2,1)S(1)} %get-tuple-element.22), channel_id=1, source_target_pairs={{0,6},{2,0},{4,2},{6,4},{1,7},{3,1},{5,3},{7,5},{8,14},{10,8},{12,... | collective-permute-start | bytes 49160 | tf_op jit(solution)/shard_map/ppermute | solution.py:163
  47.1 11.5 %collective-permute-start.9 = (bf16[16,512]{1,0:T(8,128)(2,1)S(1)}, bf16[16,512]{1,0:T(8,128)(2,1)S(1)}, u32[]{:S(2)}, u32[]{:S(2)}) collective-permute-start(bf16[16,512]{1,0:T(8,128)(2,1)S(1)} %get-tuple-element.23), channel_id=1, source_target_pairs={{0,4},{2,6},{4,0},{6,2},{1,5},{3,7},{5,1},{7,3},{8,12},{10,14},{12... | collective-permute-start | bytes 49160 | tf_op jit(solution)/shard_map/ppermute | solution.py:163
  55.2 13.8 %all-to-all-start.1 = ((bf16[8,32,512]{2,1,0:T(8,128)(2,1)}), bf16[8,32,512]{2,1,0:T(8,128)(2,1)S(1)}, u32[]{:S(2)}, u32[]{:S(2)}) async-start(bf16[8,32,512]{2,1,0:T(8,128)(2,1)} %broadcast_in_dim.6), calls=%async_computation.1 | async-start | bytes 524288 | tf_op jit(solution)/shard_map/all_to_all | solution.py:149
  60.5 5.2 %collective-permute-start.12 = (bf16[16,512]{1,0:T(8,128)(2,1)S(1)}, bf16[16,512]{1,0:T(8,128)(2,1)S(1)}, u32[]{:S(2)}, u32[]{:S(2)}) collective-permute-start(bf16[16,512]{1,0:T(8,128)(2,1)S(1)} %add_convert_fusion.14), channel_id=1, source_target_pairs={{0,4},{2,6},{4,0},{6,2},{1,5},{3,7},{5,1},{7,3},{8,12},{10,14},{12... | collective-permute-start | bytes 49160 | tf_op jit(solution)/shard_map/ppermute | solution.py:163
  69.8 18.1 %all-to-all-start.3 = ((bf16[8,64,512]{2,1,0:T(8,128)(2,1)}), bf16[8,64,512]{2,1,0:T(8,128)(2,1)S(1)}, u32[]{:S(2)}, u32[]{:S(2)}) async-start(bf16[8,64,512]{2,1,0:T(8,128)(2,1)} %broadcast_in_dim.7), calls=%async_computation.3 | async-start | bytes 1048576 | tf_op jit(solution)/shard_map/all_to_all | solution.py:149
  74.7 6.4 %collective-permute-start.7 = (bf16[256,512]{1,0:T(8,128)(2,1)S(1)}, bf16[256,512]{1,0:T(8,128)(2,1)S(1)}, u32[]{:S(2)}, u32[]{:S(2)}) collective-permute-start(bf16[256,512]{1,0:T(8,128)(2,1)S(1)} %bitcast.18), channel_id=1, source_target_pairs={{0,6},{2,0},{4,2},{6,4},{1,7},{3,1},{5,3},{7,5},{8,14},{10,8},{12,... | collective-permute-start | bytes 786440 | tf_op jit(solution)/shard_map/ppermute | solution.py:163
  75.2 8.3 %collective-permute-start.6 = (bf16[256,512]{1,0:T(8,128)(2,1)S(1)}, bf16[256,512]{1,0:T(8,128)(2,1)S(1)}, u32[]{:S(2)}, u32[]{:S(2)}) collective-permute-start(bf16[256,512]{1,0:T(8,128)(2,1)S(1)} %bitcast.19), channel_id=1, source_target_pairs={{0,4},{2,6},{4,0},{6,2},{1,5},{3,7},{5,1},{7,3},{8,12},{10,14},{12... | collective-permute-start | bytes 786440 | tf_op jit(solution)/shard_map/ppermute | solution.py:163
  76.4 9.8 %collective-permute-start.5 = (bf16[256,512]{1,0:T(8,128)(2,1)S(1)}, bf16[256,512]{1,0:T(8,128)(2,1)S(1)}, u32[]{:S(2)}, u32[]{:S(2)}) collective-permute-start(bf16[256,512]{1,0:T(8,128)(2,1)S(1)} %bitcast.20), channel_id=1, source_target_pairs={{0,2},{2,4},{4,6},{6,0},{1,3},{3,5},{5,7},{7,1},{8,10},{10,12},{12... | collective-permute-start | bytes 786440 | tf_op jit(solution)/shard_map/ppermute | solution.py:163
  88.0 19.5 %collective-permute-start.14 = (bf16[1536,512]{1,0:T(8,128)(2,1)S(1)}, bf16[1536,512]{1,0:T(8,128)(2,1)}, u32[]{:S(2)}, u32[]{:S(2)}) collective-permute-start(bf16[1536,512]{1,0:T(8,128)(2,1)S(1)} %constant_dynamic-update-slice_fusion), channel_id=1, source_target_pairs={{0,1},{1,0},{2,3},{3,2},{4,5},{5,4},{6,7},{7,6},{8,9},{9,8},{10,11... | collective-permute-start | bytes 4718600 | tf_op jit(solution)/shard_map/ppermute | solution.py:163
  94.1 5.8 %collective-permute-start.17 = (bf16[64,512]{1,0:T(8,128)(2,1)S(1)}, bf16[64,512]{1,0:T(8,128)(2,1)S(1)}, u32[]{:S(2)}, u32[]{:S(2)}) collective-permute-start(bf16[64,512]{1,0:T(8,128)(2,1)S(1)} %get-tuple-element.16), channel_id=1, source_target_pairs={{0,128},{64,192},{128,0},{192,64},{1,129},{65,193},{129,1},{193,65... | collective-permute-start | bytes 196616 | tf_op jit(solution)/shard_map/ppermute | solution.py:163
  99.9 5.0 %collective-permute-start.21 = (bf16[64,512]{1,0:T(8,128)(2,1)S(1)}, bf16[64,512]{1,0:T(8,128)(2,1)S(1)}, u32[]{:S(2)}, u32[]{:S(2)}) collective-permute-start(bf16[64,512]{1,0:T(8,128)(2,1)S(1)} %add_convert_fusion.13), channel_id=1, source_target_pairs={{0,192},{64,0},{128,64},{192,128},{1,193},{65,1},{129,65},{193,129... | collective-permute-start | bytes 196616 | tf_op jit(solution)/shard_map/ppermute | solution.py:163
  101.6 5.8 %collective-permute-start.20 = (bf16[64,512]{1,0:T(8,128)(2,1)S(1)}, bf16[64,512]{1,0:T(8,128)(2,1)S(1)}, u32[]{:S(2)}, u32[]{:S(2)}) collective-permute-start(bf16[64,512]{1,0:T(8,128)(2,1)S(1)} %add_convert_fusion.13), channel_id=1, source_target_pairs={{0,128},{64,192},{128,0},{192,64},{1,129},{65,193},{129,1},{193,65... | collective-permute-start | bytes 196616 | tf_op jit(solution)/shard_map/ppermute | solution.py:163
  111.9 5.5 %collective-permute-start.22 = (bf16[256,512]{1,0:T(8,128)(2,1)S(1)}, bf16[256,512]{1,0:T(8,128)(2,1)S(1)}, u32[]{:S(2)}, u32[]{:S(2)}) collective-permute-start(bf16[256,512]{1,0:T(8,128)(2,1)S(1)} %pad_maximum_fusion.6.mine_ref), channel_id=1, source_target_pairs={{0,1},{1,0},{2,3},{3,2},{4,5},{5,4},{6,7},{7,6},{8,9},{9,8},{10,11... | collective-permute-start | bytes 786440 | tf_op jit(solution)/shard_map/ppermute | solution.py:163
  112.1 25.7 %collective-permute-start.25 = (bf16[416,512]{1,0:T(8,128)(2,1)S(1)}, bf16[416,512]{1,0:T(8,128)(2,1)S(1)}, u32[]{:S(2)}, u32[]{:S(2)}) collective-permute-start(bf16[416,512]{1,0:T(8,128)(2,1)S(1)} %fusion.7), channel_id=1, source_target_pairs={{0,192},{64,0},{128,64},{192,128},{1,193},{65,1},{129,65},{193,129... | collective-permute-start | bytes 1277960 | tf_op jit(solution)/shard_map/ppermute | solution.py:163
  114.6 23.2 %collective-permute-start.24 = (bf16[416,512]{1,0:T(8,128)(2,1)S(1)}, bf16[416,512]{1,0:T(8,128)(2,1)S(1)}, u32[]{:S(2)}, u32[]{:S(2)}) collective-permute-start(bf16[416,512]{1,0:T(8,128)(2,1)S(1)} %fusion.7), channel_id=1, source_target_pairs={{0,64},{64,128},{128,192},{192,0},{1,65},{65,129},{129,193},{193,1... | collective-permute-start | bytes 1277960 | tf_op jit(solution)/shard_map/ppermute | solution.py:163
  114.6 23.2 %collective-permute-start.23 = (bf16[416,512]{1,0:T(8,128)(2,1)S(1)}, bf16[416,512]{1,0:T(8,128)(2,1)S(1)}, u32[]{:S(2)}, u32[]{:S(2)}) collective-permute-start(bf16[416,512]{1,0:T(8,128)(2,1)S(1)} %fusion.7), channel_id=1, source_target_pairs={{0,128},{64,192},{128,0},{192,64},{1,129},{65,193},{129,1},{193,65... | collective-permute-start | bytes 1277960 | tf_op jit(solution)/shard_map/ppermute | solution.py:163
  141.5 5.1 %collective-permute-start.27 = (f32[1,512]{1,0:T(1,128)S(1)}, f32[1,512]{1,0:T(1,128)S(1)}, u32[]{:S(2)}, u32[]{:S(2)}) collective-permute-start(f32[1,512]{1,0:T(1,128)S(1)} %add.226), channel_id=1, source_target_pairs={{0,4},{2,6},{4,0},{6,2},{1,5},{3,7},{5,1},{7,3},{8,12},{10,14},{12... | collective-permute-start | bytes 6152 | tf_op jit(solution)/shard_map/ppermute | solution.py:163
  154.8 7.5 %collective-permute-start.32 = (f32[1,512]{1,0:T(1,128)S(1)}, f32[1,512]{1,0:T(1,128)S(1)}, u32[]{:S(2)}, u32[]{:S(2)}) collective-permute-start(f32[1,512]{1,0:T(1,128)S(1)} %add.231), channel_id=1, source_target_pairs={{0,32},{8,40},{16,48},{24,56},{32,0},{40,8},{48,16},{56,24},{1,33}... | collective-permute-start | bytes 6152 | tf_op jit(solution)/shard_map/ppermute | solution.py:205
  (19 other events, 63.0 us)
